TPU v7x, 128 devices: a whole 4x4x4 slice. The times are simulated.
128 devices in a mesh: grp: 2 (over y_lo), dev: 64 (over z, x, y_hi, core).
Axes of the slice: x: 4, y: 4 (y_hi: 2, y_lo: 2; y = y_hi * 2 + y_lo), z: 4, core: 2. Of those that a mesh axis runs over, the one named last changes fastest.
Arguments:
- images: bfloat16 [114688, 1152], P(('grp', 'dev')), may hold values from -6 to 6
- texts: bfloat16 [114688, 1152], P(('grp', 'dev')), may hold values from -6 to 6
- image_partner: int32 [114688], P(('grp', 'dev')), may hold values from 0 to 114687, as said below
- text_partner: int32 [114688], P(('grp', 'dev')), may hold values from 0 to 114687, as said below
Outputs:
- grad_images: float32 [114688, 1152], P(('grp', 'dev'))
- grad_texts: float32 [114688, 1152], P(('grp', 'dev'))
Inputs may be any that keep to these rules, and one draw needn't show every extreme that they name: image_partner is a permutation of the text indices that maps each block of 896 rows onto itself. text_partner is the inverse permutation of image_partner: text_partner[image_partner[i]] == i.
All inputs are finite; a program needn't handle non-finite values.
Results may differ from a plain program's by a relative error of at most 0.0017.
Values may be sent and summed in bfloat16 or wider, within the bound.
No kernel may reach another device: no remote copies, remote signals or barrier semaphores. Data moves between devices by JAX's collectives and lax.ppermute only.
A program may use at most 128 MiB of HBM per device.

v0:
```python
import functools

import jax
import jax.numpy as jnp
from jax import lax
from jax.experimental import pallas as pl
from jax.experimental.pallas import tpu as pltpu
from jax.sharding import PartitionSpec as P

AXES = ("grp", "dev")
LOG2E = 1.4426950408889634
NT = (((1,), (1,)), ((), ()))
BLOCK = 448
STEP = 256
PIECES = (288, 288, 192, 128)
DEVICES = range(128)
NO_COVER = pl.CostEstimate(flops=1, bytes_accessed=1, transcendentals=0)


CORE_SWAP = [(d, d ^ 1) for d in DEVICES]
HALF_SWAP = [(d, d ^ 2) for d in DEVICES]
HAND_ON = [(d, (d + 4 if d & 2 == 0 else d - 4) % 128) for d in DEVICES]
HAND_ON_WITHIN = [(d, to) for d, to in HAND_ON if (d >> 6) == (to >> 6)]
AHEAD = [(d, (d - 2) % 128) for d in DEVICES]
BEHIND = [(d, (d + 2) % 128) for d in DEVICES]


ACROSS = [(62, 64), (63, 65), (64, 62), (65, 63), (126, 0), (127, 1), (0, 126), (1, 127)]


def weights(product, temp, positive):
    exponent = product * (-temp * LOG2E) + 2.0 * LOG2E
    if positive is None:
        return (temp / (1.0 + jnp.exp2(exponent))).astype(jnp.bfloat16)
    exponent = jnp.where(positive, -exponent, exponent)
    return (jnp.where(positive, -temp, temp) / (1.0 + jnp.exp2(exponent))).astype(jnp.bfloat16)


def gradient(left, stack, weight, temp, partner):
    many = stack.shape[0]
    for at in range(0, many, STEP):
        end = min(many, at + STEP)
        product = lax.dot_general(left, stack[at:end, :], NT, preferred_element_type=jnp.float32)
        positive = None
        if partner is not None and at < many // 2:
            positive = partner == at + lax.broadcasted_iota(jnp.int32, product.shape, 1)
        weight[:, at:end] = weights(product, temp, positive)
    return jnp.dot(weight[...], stack[...], preferred_element_type=jnp.float32)


def own_body(temp, waits, rows, own, other, partner, *refs):
    total, kept, token, stack, weight, sems = refs[waits:]
    token[...] = jnp.zeros_like(token)
    height = kept.shape[0]
    copies = [
        pltpu.make_async_copy(rows, kept, sems.at[0]),
        pltpu.make_async_copy(own, stack.at[pl.ds(0, height)], sems.at[1]),
        pltpu.make_async_copy(other, stack.at[pl.ds(height, height)], sems.at[2]),
    ]
    for copy in copies:
        copy.start()
    for copy in copies:
        copy.wait()
    for b in range(height // BLOCK):
        here = slice(b * BLOCK, (b + 1) * BLOCK)
        total[here, :] = gradient(kept[here, :], stack, weight.at[b % 2], temp, partner[here, :])


TOKEN = jax.ShapeDtypeStruct((8, 128), jnp.float32)


def behind(array, token):
    return array + token[0, 0].astype(array.dtype)


def in_hbm(*arrays):
    return [pltpu.with_memory_space_constraint(array, pltpu.HBM) for array in arrays]


def own_gradient(rows, own, other, partner, temp, waits):
    height, width = rows.shape
    hbm, vmem = pl.BlockSpec(memory_space=pltpu.HBM), pl.BlockSpec(memory_space=pltpu.VMEM)
    return pl.pallas_call(
        functools.partial(own_body, temp, len(waits)),
        in_specs=[hbm, hbm, hbm, vmem] + [hbm] * len(waits),
        out_specs=[vmem, vmem, vmem],
        out_shape=[
            pltpu.VMEM((height, width), jnp.float32),
            pltpu.VMEM((height, width), rows.dtype),
            TOKEN,
        ],
        scratch_shapes=[
            pltpu.VMEM((2 * height, width), rows.dtype),
            pltpu.VMEM((2, BLOCK, 2 * height), jnp.bfloat16),
            pltpu.SemaphoreType.DMA((3,)),
        ],
        compiler_params=pltpu.CompilerParams(vmem_limit_bytes=14 * 2**20),
        cost_estimate=pl.CostEstimate(
            flops=8 * height * height * width, bytes_accessed=6 * height * width, transcendentals=4 * height * height
        ),
    )(*in_hbm(rows, own, other), partner, *in_hbm(*waits))


def visit_body(sizes, temp, last, waits, *refs):
    count = len(sizes)
    kept, before, others = refs[:2], refs[2:4], refs[4 : 4 + count]
    refs = refs[4 + count + waits :]
    out, (token, stack, weight, sems, *rest) = refs[:2], refs[2:]
    token[...] = jnp.zeros_like(token)
    copies = []
    for side in (0, 1):
        at = 0
        for i, size in enumerate(sizes):
            source = others[i].at[pl.ds(side * size, size)]
            copies.append(pltpu.make_async_copy(source, stack.at[side, pl.ds(at, size)], sems.at[side, i]))
            at += size
    for copy in copies:
        copy.start()
    sent = []
    for side in (0, 1):
        for copy in copies[side * count : (side + 1) * count]:
            copy.wait()
        for b in range(kept[side].shape[0] // BLOCK):
            here = slice(b * BLOCK, (b + 1) * BLOCK)
            grads = gradient(kept[side][here, :], stack.at[side], weight.at[b % 2], temp, None)
            if not last:
                out[side][here, :] = before[side][here, :] + grads
                continue
            result, result_sems = rest
            result[side, here, :] = before[side][here, :] + grads
            rows = pl.ds(b * BLOCK, BLOCK)
            copy = pltpu.make_async_copy(result.at[side, rows], out[side].at[rows], result_sems.at[side, b])
            copy.start()
            sent.append(copy)
    for copy in sent:
        copy.wait()


def visit(kept, before, others, temp, last, waits):
    height, width = kept[0].shape
    sizes = tuple(other.shape[0] // 2 for other in others)
    many, count = sum(sizes), len(sizes)
    hbm, vmem = pl.BlockSpec(memory_space=pltpu.HBM), pl.BlockSpec(memory_space=pltpu.VMEM)
    kept = [pltpu.with_memory_space_constraint(array, pltpu.VMEM) for array in kept]
    before = [pltpu.with_memory_space_constraint(array, pltpu.VMEM) for array in before]
    scratch = [
        pltpu.VMEM((2, many, width), kept[0].dtype),
        pltpu.VMEM((2, BLOCK, many), jnp.bfloat16),
        pltpu.SemaphoreType.DMA((2, count)),
    ]
    if last:
        out_shape = [jax.ShapeDtypeStruct((height, width), jnp.float32)] * 2
        scratch += [pltpu.VMEM((2, height, width), jnp.float32), pltpu.SemaphoreType.DMA((2, height // BLOCK))]
    else:
        out_shape = [pltpu.VMEM((height, width), jnp.float32)] * 2
    return pl.pallas_call(
        functools.partial(visit_body, sizes, temp, last, len(waits)),
        in_specs=[vmem] * 4 + [hbm] * (count + len(waits)),
        out_specs=[hbm if last else vmem] * 2 + [vmem],
        out_shape=out_shape + [TOKEN],
        scratch_shapes=scratch,
        input_output_aliases={} if last else {2: 0, 3: 1},
        compiler_params=pltpu.CompilerParams(vmem_limit_bytes=14 * 2**20),
        cost_estimate=pl.CostEstimate(
            flops=8 * height * many * width, bytes_accessed=4 * many * width, transcendentals=4 * height * many
        ),
    )(*kept, *before, *in_hbm(*others, *waits))


def shards(images, texts, image_partner, text_partner):
    height, width = images.shape
    temp = 2.0 * width ** (-0.5)
    index = lax.axis_index(AXES)
    even = (index & 1) == 0
    first_passes_on = (index & 1) == ((index >> 1) & 1)
    pieces = []
    at = 0
    for size in PIECES:
        pieces.append(jnp.concatenate([texts[at : at + size], images[at : at + size]], axis=0))
        at += size

    partner_texts = lax.ppermute(texts, AXES, CORE_SWAP)
    partner_images = lax.ppermute(images, AXES, CORE_SWAP)
    one = [lax.ppermute(piece, AXES, HALF_SWAP) for piece in pieces[:2]]
    across = [lax.ppermute(rows, AXES, ACROSS) for rows in (pieces[1][: PIECES[1]], pieces[1][PIECES[1] :])]

    start = index * height
    total_images, kept_images, token = own_gradient(
        images, texts, partner_texts, (image_partner - start)[:, None], temp, (pieces[2], pieces[3])
    )
    total_texts, kept_texts, token = own_gradient(
        texts, images, partner_images, (text_partner - start)[:, None], temp, (token, across[0])
    )
    kept, totals = (kept_images, kept_texts), (total_images, total_texts)

    two = [lax.ppermute(one[0], AXES, HAND_ON), lax.ppermute(one[1], AXES, HAND_ON_WITHIN)]
    ahead = [lax.ppermute(piece, AXES, AHEAD) for piece in pieces[2:]]
    back = [lax.ppermute(piece, AXES, BEHIND) for piece in pieces[2:]]

    near = lax.ppermute(behind(jnp.where(first_passes_on, one[0], two[0]), token), AXES, CORE_SWAP)
    *totals, token = visit(kept, totals, [one[0], two[0], near], temp, False, (across[1],))
    near = lax.ppermute(behind(jnp.where(even, ahead[0], back[0]), token), AXES, CORE_SWAP)
    two[1] = behind(two[1] + jnp.concatenate(across, axis=0), token)
    far = lax.ppermute(jnp.where(first_passes_on, one[1], two[1]), AXES, CORE_SWAP)
    *totals, token = visit(kept, totals, [ahead[0], back[0], near, one[1], two[1], far], temp, False, ())
    near = lax.ppermute(behind(jnp.where(even, ahead[1], back[1]), token), AXES, CORE_SWAP)
    *totals, token = visit(kept, totals, [ahead[1], back[1], near], temp, True, ())
    return tuple(totals)


def solution(mesh):
    return jax.shard_map(
        shards,
        mesh=mesh,
        in_specs=(P(AXES, None), P(AXES, None), P(AXES), P(AXES)),
        out_specs=(P(AXES, None), P(AXES, None)),
        check_vma=False,
    )
```

profile of v0, /device:TPU:105, one launch (start us, length us, event | category | flops | bytes accessed | tf_op | source)
XLA Modules:
  0.0 195.8 jit_solution(10099652178305439254)
XLA Ops:
  1.5 2.2 %fusion.3 = (bf16[288,1152]{1,0:T(8,128)(2,1)S(1)}, bf16[288,1152]{1,0:T(8,128)(2,1)}) fusion(bf16[896,1152]{1,0:T(8,128)(2,1)} %rows.3), kind=kLoop, calls=%fused_computation.13 | loop fusion | bytes 2654208 | tf_op jit(solution)/shard_map/slice | solution.py:179
  3.8 1.3 pad_maximum_fusion
  5.1 2.0 %collective-permute-start.3 = (bf16[576,1152]{1,0:T(8,128)(2,1)}, bf16[576,1152]{1,0:T(8,128)(2,1)}, u32[]{:S(2)}, u32[]{:S(2)}) collective-permute-start(bf16[576,1152]{1,0:T(8,128)(2,1)} %pad_maximum_fusion), channel_id=1, source_target_pairs={{0,2},{1,3},{2,0},{3,1},{4,6},{5,7},{6,4},{7,5},{8,10},{9,11},{10,... | collective-permute-start | bytes 3981320 | tf_op jit(solution)/shard_map/ppermute | solution.py:184
  7.1 1.5 collective-permute-start.2
  8.6 2.4 %pad_maximum_fusion.1 = bf16[576,1152]{1,0:T(8,128)(2,1)} fusion(bf16[288,1152]{1,0:T(8,128)(2,1)S(1)} %get-tuple-element.32, bf16[288,1152]{1,0:T(8,128)(2,1)} %get-tuple-element.35), kind=kLoop, calls=%fused_computation.1 | loop fusion | flops 2654208 | bytes 2654208 | tf_op jit(solution)/shard_map/concatenate | solution.py:179
  16.3 35.0 %collective-permute-done.3.refs_4_ = bf16[576,1152]{1,0:T(8,128)(2,1)} collective-permute-done((bf16[576,1152]{1,0:T(8,128)(2,1)}, bf16[576,1152]{1,0:T(8,128)(2,1)}, u32[]{:S(2)}, u32[]{:S(2)}) %collective-permute-start.3) | collective-permute-done | bytes 1327136 | tf_op jit(solution)/shard_map/ppermute | solution.py:184
  51.5 12.0 %shard_map.59 = (f32[896,1152]{1,0:T(8,128)S(1)}, bf16[896,1152]{1,0:T(8,128)(2,1)S(1)}, f32[8,128]{1,0:T(8,128)S(1)}) custom-call(bf16[896,1152]{1,0:T(8,128)(2,1)} %own.3, bf16[896,1152]{1,0:T(8,128)(2,1)} %rows.3, bf16[896,1152]{1,0:T(8,128)(2,1)} %collective-permute-done.other, s32[896,1]{1,0:T(8,128)S(1)} %broadcast_in_dim.8.partner, ...), custom_call_target="tpu_custom_call" | custom-call | flops 7398752256 | bytes 6193152 | tf_op jit(solution)/shard_map/pallas_call | solution.py:83
  63.5 2.0 %copy-done = f32[896,1152]{1,0:T(8,128)} copy-done((f32[896,1152]{1,0:T(8,128)}, f32[896,1152]{1,0:T(8,128)S(1)}, u32[]{:S(2)}) %copy-start) | copy-done | bytes 4128792
  66.1 12.4 %shard_map.60 = (f32[896,1152]{1,0:T(8,128)S(1)}, bf16[896,1152]{1,0:T(8,128)(2,1)S(1)}, f32[8,128]{1,0:T(8,128)S(1)}) custom-call(bf16[896,1152]{1,0:T(8,128)(2,1)} %rows.3, bf16[896,1152]{1,0:T(8,128)(2,1)} %own.3, bf16[896,1152]{1,0:T(8,128)(2,1)} %collective-permute-done.1.other, s32[896,1]{1,0:T(8,128)S(1)} %broadcast_in_dim.9.partner, ...), custom_call_target="tpu_custom_call" | custom-call | flops 7398752256 | bytes 6193152 | tf_op jit(solution)/shard_map/pallas_call | solution.py:83
  78.5 2.0 %copy-done.4 = f32[896,1152]{1,0:T(8,128)} copy-done((f32[896,1152]{1,0:T(8,128)}, f32[896,1152]{1,0:T(8,128)S(1)}, u32[]{:S(2)}) %copy-start.4) | copy-done | bytes 4128792
  80.5 1.3 copy-done.8
  82.4 1.9 select_add_fusion
  84.3 4.3 %collective-permute-start.5 = (bf16[576,1152]{1,0:T(8,128)(2,1)}, bf16[576,1152]{1,0:T(8,128)(2,1)}, u32[]{:S(2)}, u32[]{:S(2)}) collective-permute-start(bf16[576,1152]{1,0:T(8,128)(2,1)} %select_add_fusion), channel_id=1, source_target_pairs={{0,1},{1,0},{2,3},{3,2},{4,5},{5,4},{6,7},{7,6},{8,9},{9,8},{10,11... | collective-permute-start | bytes 3981320 | tf_op jit(solution)/shard_map/ppermute | solution.py:200
  89.3 3.0 %collective-permute-done.10.refs_7_ = bf16[576,1152]{1,0:T(8,128)(2,1)} collective-permute-done((bf16[576,1152]{1,0:T(8,128)(2,1)}, bf16[576,1152]{1,0:T(8,128)(2,1)}, u32[]{:S(2)}, u32[]{:S(2)}) %collective-permute-start.10) | collective-permute-done | bytes 1327136 | tf_op jit(solution)/shard_map/ppermute | solution.py:184
  92.4 1.9 collective-permute-start.11
  94.4 3.8 %collective-permute-start.8 = (bf16[384,1152]{1,0:T(8,128)(2,1)}, bf16[384,1152]{1,0:T(8,128)(2,1)}, u32[]{:S(2)}, u32[]{:S(2)}) collective-permute-start(bf16[384,1152]{1,0:T(8,128)(2,1)} %pad_maximum_fusion.2.refs_0_), channel_id=1, source_target_pairs={{0,2},{1,3},{2,4},{3,5},{4,6},{5,7},{6,8},{7,9},{8,10},{9,11},{10,... | collective-permute-start | bytes 2654216 | tf_op jit(solution)/shard_map/ppermute | solution.py:198
  99.0 2.2 %copy-done.1 = f32[896,1152]{1,0:T(8,128)S(1)} copy-done((f32[896,1152]{1,0:T(8,128)S(1)}, f32[896,1152]{1,0:T(8,128)}, u32[]{:S(2)}) %copy-start.1) | copy-done | bytes 4128792
  101.2 2.2 %copy-done.5 = f32[896,1152]{1,0:T(8,128)S(1)} copy-done((f32[896,1152]{1,0:T(8,128)S(1)}, f32[896,1152]{1,0:T(8,128)}, u32[]{:S(2)}) %copy-start.5) | copy-done | bytes 4128792
  103.4 1.6 copy-done.9
  104.9 11.8 %shard_map.61 = (f32[896,1152]{1,0:T(8,128)S(1)}, f32[896,1152]{1,0:T(8,128)S(1)}, f32[8,128]{1,0:T(8,128)S(1)}) custom-call(bf16[896,1152]{1,0:T(8,128)(2,1)S(1)} %get-tuple-element.16.refs_0_, bf16[896,1152]{1,0:T(8,128)(2,1)S(1)} %copy-done.9, f32[896,1152]{1,0:T(8,128)S(1)} %copy-done.1, ...), custom_call_target="tpu_custom_call", output_to_operand_aliasing={{0}: (2, {}), {1}: (3, {})} | custom-call | flops 7134511104 | bytes 3981312 | tf_op jit(solution)/shard_map/pallas_call | solution.py:156
  116.7 2.0 %copy-done.2 = f32[896,1152]{1,0:T(8,128)} copy-done((f32[896,1152]{1,0:T(8,128)}, f32[896,1152]{1,0:T(8,128)S(1)}, u32[]{:S(2)}) %copy-start.2) | copy-done | bytes 4128792
  118.7 2.0 %copy-done.6 = f32[896,1152]{1,0:T(8,128)} copy-done((f32[896,1152]{1,0:T(8,128)}, f32[896,1152]{1,0:T(8,128)S(1)}, u32[]{:S(2)}) %copy-start.6) | copy-done | bytes 4128792
  121.3 23.6 %collective-permute-done.11 = bf16[576,1152]{1,0:T(8,128)(2,1)} collective-permute-done((bf16[576,1152]{1,0:T(8,128)(2,1)}, bf16[576,1152]{1,0:T(8,128)(2,1)}, u32[]{:S(2)}, u32[]{:S(2)}) %collective-permute-start.11) | collective-permute-done | bytes 1327136 | tf_op jit(solution)/shard_map/ppermute | solution.py:196
  144.9 4.7 %broadcast_select_fusion = (bf16[576,1152]{1,0:T(8,128)(2,1)S(1)}, bf16[576,1152]{1,0:T(8,128)(2,1)}) fusion(bf16[576,1152]{1,0:T(8,128)(2,1)} %collective-permute-done.10.refs_7_, pred[]{:T(512)S(6)} %eq.6, bf16[]{:T(256)} %bitcast.1, bf16[576,1152]{1,0:T(8,128)(2,1)} %collective-permute-done.11, bf16[288,1152]{1,0:T(8,128)(2,1)} %copy-done.18, ...), kind=kLoop, calls=%fused_computation.5 | loop fusion | flops 5971968 | bytes 6635523 | tf_op jit(solution)/shard_map/jit(_where)/select_n | solution.py:204
  149.6 2.9 %collective-permute-start.12 = (bf16[576,1152]{1,0:T(8,128)(2,1)S(1)}, bf16[576,1152]{1,0:T(8,128)(2,1)S(1)}, u32[]{:S(2)}, u32[]{:S(2)}) collective-permute-start(bf16[576,1152]{1,0:T(8,128)(2,1)S(1)} %get-tuple-element.30), channel_id=1, source_target_pairs={{0,1},{1,0},{2,3},{3,2},{4,5},{5,4},{6,7},{7,6},{8,9},{9,8},{10,11... | collective-permute-start | bytes 3981320 | tf_op jit(solution)/shard_map/ppermute | solution.py:204
  152.5 2.0 %select_add_fusion.1 = bf16[384,1152]{1,0:T(8,128)(2,1)S(1)} fusion(bf16[384,1152]{1,0:T(8,128)(2,1)} %collective-permute-done.7.refs_4_, bf16[384,1152]{1,0:T(8,128)(2,1)} %collective-permute-done.8.refs_5_, pred[]{:T(512)S(6)} %eq.7, bf16[]{:T(256)} %bitcast.1), kind=kLoop, calls=%fused_computation.7 | loop fusion | flops 884736 | bytes 2654211 | tf_op jit(solution)/shard_map/add | solution.py:73
  154.6 2.3 %collective-permute-start.13 = (bf16[256,1152]{1,0:T(8,128)(2,1)S(1)}, bf16[256,1152]{1,0:T(8,128)(2,1)S(1)}, u32[]{:S(2)}, u32[]{:S(2)}) collective-permute-start(bf16[256,1152]{1,0:T(8,128)(2,1)S(1)} %copy-done.20), channel_id=1, source_target_pairs={{0,126},{1,127},{2,0},{3,1},{4,2},{5,3},{6,4},{7,5},{8,6},{9,7},{1... | collective-permute-start | bytes 1769480 | tf_op jit(solution)/shard_map/ppermute | solution.py:197
  159.0 19.4 %shard_map.62 = (f32[896,1152]{1,0:T(8,128)S(1)}, f32[896,1152]{1,0:T(8,128)S(1)}, f32[8,128]{1,0:T(8,128)S(1)}) custom-call(bf16[896,1152]{1,0:T(8,128)(2,1)S(1)} %get-tuple-element.16.refs_0_, bf16[896,1152]{1,0:T(8,128)(2,1)S(1)} %copy-done.10, f32[896,1152]{1,0:T(8,128)S(1)} %copy-done.3, ...), custom_call_target="tpu_custom_call", output_to_operand_aliasing={{0}: (2, {}), {1}: (3, {})} | custom-call | flops 11890851840 | bytes 6635520 | tf_op jit(solution)/shard_map/pallas_call | solution.py:156
  179.0 3.4 %collective-permute-done.13.refs_4_ = bf16[256,1152]{1,0:T(8,128)(2,1)S(1)} collective-permute-done((bf16[256,1152]{1,0:T(8,128)(2,1)S(1)}, bf16[256,1152]{1,0:T(8,128)(2,1)S(1)}, u32[]{:S(2)}, u32[]{:S(2)}) %collective-permute-start.13) | collective-permute-done | bytes 589856 | tf_op jit(solution)/shard_map/ppermute | solution.py:197
  183.1 1.4 collective-permute-start.15
  184.5 1.6 collective-permute-done.15.refs_6_
  187.0 8.6 %shard_map.63 = (f32[896,1152]{1,0:T(8,128)}, f32[896,1152]{1,0:T(8,128)}, f32[8,128]{1,0:T(8,128)}) custom-call(bf16[896,1152]{1,0:T(8,128)(2,1)S(1)} %get-tuple-element.16.refs_0_, bf16[896,1152]{1,0:T(8,128)(2,1)S(1)} %copy-done.10, f32[896,1152]{1,0:T(8,128)S(1)} %get-tuple-element.25.refs_2_, f32[896,1152]{1,0:T(8,128)S(1)} %get-tuple-element.26.refs_3_, ...), custom_call_target="tpu_custom_call" | custom-call | flops 3170893824 | bytes 1769472 | tf_op jit(solution)/shard_map/pallas_call | solution.py:156
  (79 shorter events, 14.1 us)
Async XLA Ops:
  0.6 3.1 %copy-start.16 = (bf16[896,1152]{1,0:T(8,128)(2,1)S(1)}, bf16[896,1152]{1,0:T(8,128)(2,1)}, u32[]{:S(2)}) copy-start(bf16[896,1152]{1,0:T(8,128)(2,1)} %own.3) | copy-start | bytes 6193156
  0.6 50.9 %collective-permute-start = (bf16[896,1152]{1,0:T(8,128)(2,1)}, bf16[896,1152]{1,0:T(8,128)(2,1)}, u32[]{:S(2)}, u32[]{:S(2)}) collective-permute-start(bf16[896,1152]{1,0:T(8,128)(2,1)} %rows.3), channel_id=1, source_target_pairs={{0,1},{1,0},{2,3},{3,2},{4,5},{5,4},{6,7},{7,6},{8,9},{9,8},{10,11... | collective-permute-start | bytes 6193160 | tf_op jit(solution)/shard_map/ppermute | solution.py:182
  1.4 64.7 %collective-permute-start.1 = (bf16[896,1152]{1,0:T(8,128)(2,1)}, bf16[896,1152]{1,0:T(8,128)(2,1)}, u32[]{:S(2)}, u32[]{:S(2)}) collective-permute-start(bf16[896,1152]{1,0:T(8,128)(2,1)} %own.3), channel_id=1, source_target_pairs={{0,1},{1,0},{2,3},{3,2},{4,5},{5,4},{6,7},{7,6},{8,9},{9,8},{10,11... | collective-permute-start | bytes 6193160 | tf_op jit(solution)/shard_map/ppermute | solution.py:183
  3.8 7.1 %copy-start.12 = (bf16[288,1152]{1,0:T(8,128)(2,1)}, bf16[288,1152]{1,0:T(8,128)(2,1)S(1)}, u32[]{:S(2)}) copy-start(bf16[288,1152]{1,0:T(8,128)(2,1)S(1)} %get-tuple-element.32) | copy-start | bytes 1990660
  5.1 46.2 %collective-permute-start.3 = (bf16[576,1152]{1,0:T(8,128)(2,1)}, bf16[576,1152]{1,0:T(8,128)(2,1)}, u32[]{:S(2)}, u32[]{:S(2)}) collective-permute-start(bf16[576,1152]{1,0:T(8,128)(2,1)} %pad_maximum_fusion), channel_id=1, source_target_pairs={{0,2},{1,3},{2,0},{3,1},{4,6},{5,7},{6,4},{7,5},{8,10},{9,11},{10,... | collective-permute-start | bytes 3981320 | tf_op jit(solution)/shard_map/ppermute | solution.py:184
  7.1 59.0 %collective-permute-start.2 = (bf16[288,1152]{1,0:T(8,128)(2,1)}, bf16[288,1152]{1,0:T(8,128)(2,1)}, u32[]{:S(2)}, u32[]{:S(2)}) collective-permute-start(bf16[288,1152]{1,0:T(8,128)(2,1)} %get-tuple-element.35), channel_id=1, source_target_pairs={{62,64},{63,65},{64,62},{65,63},{126,0},{127,1},{0,126},{1,127}} | collective-permute-start | bytes 1990664 | tf_op jit(solution)/shard_map/ppermute | solution.py:185
  11.0 3.1 %copy-start.21 = (s32[896]{0:T(1024)S(1)}, s32[896]{0:T(1024)}, u32[]{:S(2)}) copy-start(s32[896]{0:T(1024)} %param.6) | copy-start | bytes 10756
  11.0 3.3 %copy-start.22 = (s32[896]{0:T(1024)S(1)}, s32[896]{0:T(1024)}, u32[]{:S(2)}) copy-start(s32[896]{0:T(1024)} %param.7) | copy-start | bytes 10756
  11.0 81.4 %collective-permute-start.10 = (bf16[576,1152]{1,0:T(8,128)(2,1)}, bf16[576,1152]{1,0:T(8,128)(2,1)}, u32[]{:S(2)}, u32[]{:S(2)}) collective-permute-start(bf16[576,1152]{1,0:T(8,128)(2,1)} %pad_maximum_fusion.1), channel_id=1, source_target_pairs={{0,2},{1,3},{2,0},{3,1},{4,6},{5,7},{6,4},{7,5},{8,10},{9,11},{10,... | collective-permute-start | bytes 3981320 | tf_op jit(solution)/shard_map/ppermute | solution.py:184
  51.3 31.0 %collective-permute-start.4 = (bf16[576,1152]{1,0:T(8,128)(2,1)}, bf16[576,1152]{1,0:T(8,128)(2,1)S(1)}, u32[]{:S(2)}, u32[]{:S(2)}) collective-permute-start(bf16[576,1152]{1,0:T(8,128)(2,1)} %collective-permute-done.3.refs_4_), channel_id=1, source_target_pairs={{0,4},{1,5},{2,126},{3,127},{4,8},{5,9},{6,2},{7,3},{8,12},{9,13},... | collective-permute-start | bytes 3981320 | tf_op jit(solution)/shard_map/ppermute | solution.py:196
  63.5 2.0 %copy-start = (f32[896,1152]{1,0:T(8,128)}, f32[896,1152]{1,0:T(8,128)S(1)}, u32[]{:S(2)}) copy-start(f32[896,1152]{1,0:T(8,128)S(1)} %get-tuple-element.19.refs_2_) | copy-start | bytes 12386308
  78.5 2.0 %copy-start.4 = (f32[896,1152]{1,0:T(8,128)}, f32[896,1152]{1,0:T(8,128)S(1)}, u32[]{:S(2)}) copy-start(f32[896,1152]{1,0:T(8,128)S(1)} %get-tuple-element.20.refs_3_) | copy-start | bytes 12386308
  82.4 6.3 %copy-start.13 = (bf16[288,1152]{1,0:T(8,128)(2,1)S(1)}, bf16[288,1152]{1,0:T(8,128)(2,1)}, u32[]{:S(2)}) copy-start(bf16[288,1152]{1,0:T(8,128)(2,1)} %copy-done.12) | copy-start | bytes 1990660
  84.3 13.8 %collective-permute-start.5 = (bf16[576,1152]{1,0:T(8,128)(2,1)}, bf16[576,1152]{1,0:T(8,128)(2,1)}, u32[]{:S(2)}, u32[]{:S(2)}) collective-permute-start(bf16[576,1152]{1,0:T(8,128)(2,1)} %select_add_fusion), channel_id=1, source_target_pairs={{0,1},{1,0},{2,3},{3,2},{4,5},{5,4},{6,7},{7,6},{8,9},{9,8},{10,11... | collective-permute-start | bytes 3981320 | tf_op jit(solution)/shard_map/ppermute | solution.py:200
  88.6 9.5 %collective-permute-start.6 = (bf16[288,1152]{1,0:T(8,128)(2,1)S(1)}, bf16[288,1152]{1,0:T(8,128)(2,1)S(1)}, u32[]{:S(2)}, u32[]{:S(2)}) collective-permute-start(bf16[288,1152]{1,0:T(8,128)(2,1)S(1)} %copy-done.13), channel_id=1, source_target_pairs={{62,64},{63,65},{64,62},{65,63},{126,0},{127,1},{0,126},{1,127}} | collective-permute-start | bytes 1990664 | tf_op jit(solution)/shard_map/ppermute | solution.py:185
  92.4 52.5 %collective-permute-start.11 = (bf16[576,1152]{1,0:T(8,128)(2,1)}, bf16[576,1152]{1,0:T(8,128)(2,1)}, u32[]{:S(2)}, u32[]{:S(2)}) collective-permute-start(bf16[576,1152]{1,0:T(8,128)(2,1)} %collective-permute-done.10.refs_7_), channel_id=1, source_target_pairs={{0,4},{1,5},{4,8},{5,9},{6,2},{7,3},{8,12},{9,13},{10,6},{11,7},{1... | collective-permute-start | bytes 3981320 | tf_op jit(solution)/shard_map/ppermute | solution.py:196
  94.3 58.2 %collective-permute-start.7 = (bf16[384,1152]{1,0:T(8,128)(2,1)}, bf16[384,1152]{1,0:T(8,128)(2,1)}, u32[]{:S(2)}, u32[]{:S(2)}) collective-permute-start(bf16[384,1152]{1,0:T(8,128)(2,1)} %pad_maximum_fusion.2.refs_0_), channel_id=1, source_target_pairs={{0,126},{1,127},{2,0},{3,1},{4,2},{5,3},{6,4},{7,5},{8,6},{9,7},{1... | collective-permute-start | bytes 2654216 | tf_op jit(solution)/shard_map/ppermute | solution.py:197
  94.4 58.1 %collective-permute-start.8 = (bf16[384,1152]{1,0:T(8,128)(2,1)}, bf16[384,1152]{1,0:T(8,128)(2,1)}, u32[]{:S(2)}, u32[]{:S(2)}) collective-permute-start(bf16[384,1152]{1,0:T(8,128)(2,1)} %pad_maximum_fusion.2.refs_0_), channel_id=1, source_target_pairs={{0,2},{1,3},{2,4},{3,5},{4,6},{5,7},{6,8},{7,9},{8,10},{9,11},{10,... | collective-permute-start | bytes 2654216 | tf_op jit(solution)/shard_map/ppermute | solution.py:198
  99.0 2.2 %copy-start.1 = (f32[896,1152]{1,0:T(8,128)S(1)}, f32[896,1152]{1,0:T(8,128)}, u32[]{:S(2)}) copy-start(f32[896,1152]{1,0:T(8,128)} %copy-done) | copy-start | bytes 12386308
  101.2 2.2 %copy-start.5 = (f32[896,1152]{1,0:T(8,128)S(1)}, f32[896,1152]{1,0:T(8,128)}, u32[]{:S(2)}) copy-start(f32[896,1152]{1,0:T(8,128)} %copy-done.4) | copy-start | bytes 12386308
  104.9 54.1 %copy-start.10 = (bf16[896,1152]{1,0:T(8,128)(2,1)S(1)}, bf16[896,1152]{1,0:T(8,128)(2,1)}, u32[]{:S(2)}) copy-start(bf16[896,1152]{1,0:T(8,128)(2,1)} %copy-done.8) | copy-start | bytes 6193156
  116.7 2.0 %copy-start.2 = (f32[896,1152]{1,0:T(8,128)}, f32[896,1152]{1,0:T(8,128)S(1)}, u32[]{:S(2)}) copy-start(f32[896,1152]{1,0:T(8,128)S(1)} %get-tuple-element.22.refs_2_) | copy-start | bytes 12386308
  144.9 14.1 %copy-start.3 = (f32[896,1152]{1,0:T(8,128)S(1)}, f32[896,1152]{1,0:T(8,128)}, u32[]{:S(2)}) copy-start(f32[896,1152]{1,0:T(8,128)} %copy-done.2) | copy-start | bytes 12386308
  144.9 14.1 %copy-start.7 = (f32[896,1152]{1,0:T(8,128)S(1)}, f32[896,1152]{1,0:T(8,128)}, u32[]{:S(2)}) copy-start(f32[896,1152]{1,0:T(8,128)} %copy-done.6) | copy-start | bytes 12386308
  149.6 5.0 %copy-start.20 = (bf16[256,1152]{1,0:T(8,128)(2,1)S(1)}, bf16[256,1152]{1,0:T(8,128)(2,1)}, u32[]{:S(2)}) copy-start(bf16[256,1152]{1,0:T(8,128)(2,1)} %pad_maximum_fusion.3.refs_1_) | copy-start | bytes 1769476
  149.6 8.0 %collective-permute-start.12 = (bf16[576,1152]{1,0:T(8,128)(2,1)S(1)}, bf16[576,1152]{1,0:T(8,128)(2,1)S(1)}, u32[]{:S(2)}, u32[]{:S(2)}) collective-permute-start(bf16[576,1152]{1,0:T(8,128)(2,1)S(1)} %get-tuple-element.30), channel_id=1, source_target_pairs={{0,1},{1,0},{2,3},{3,2},{4,5},{5,4},{6,7},{7,6},{8,9},{9,8},{10,11... | collective-permute-start | bytes 3981320 | tf_op jit(solution)/shard_map/ppermute | solution.py:204
  154.5 3.1 %collective-permute-start.9 = (bf16[384,1152]{1,0:T(8,128)(2,1)S(1)}, bf16[384,1152]{1,0:T(8,128)(2,1)S(1)}, u32[]{:S(2)}, u32[]{:S(2)}) collective-permute-start(bf16[384,1152]{1,0:T(8,128)(2,1)S(1)} %select_add_fusion.1), channel_id=1, source_target_pairs={{0,1},{1,0},{2,3},{3,2},{4,5},{5,4},{6,7},{7,6},{8,9},{9,8},{10,11... | collective-permute-start | bytes 2654216 | tf_op jit(solution)/shard_map/ppermute | solution.py:202
  154.6 27.8 %collective-permute-start.13 = (bf16[256,1152]{1,0:T(8,128)(2,1)S(1)}, bf16[256,1152]{1,0:T(8,128)(2,1)S(1)}, u32[]{:S(2)}, u32[]{:S(2)}) collective-permute-start(bf16[256,1152]{1,0:T(8,128)(2,1)S(1)} %copy-done.20), channel_id=1, source_target_pairs={{0,126},{1,127},{2,0},{3,1},{4,2},{5,3},{6,4},{7,5},{8,6},{9,7},{1... | collective-permute-start | bytes 1769480 | tf_op jit(solution)/shard_map/ppermute | solution.py:197
  156.9 25.5 %collective-permute-start.14 = (bf16[256,1152]{1,0:T(8,128)(2,1)S(1)}, bf16[256,1152]{1,0:T(8,128)(2,1)S(1)}, u32[]{:S(2)}, u32[]{:S(2)}) collective-permute-start(bf16[256,1152]{1,0:T(8,128)(2,1)S(1)} %copy-done.20), channel_id=1, source_target_pairs={{0,2},{1,3},{2,4},{3,5},{4,6},{5,7},{6,8},{7,9},{8,10},{9,11},{10,... | collective-permute-start | bytes 1769480 | tf_op jit(solution)/shard_map/ppermute | solution.py:198
  182.4 3.8 %copy-start.14 = (bf16[256,1152]{1,0:T(8,128)(2,1)}, bf16[256,1152]{1,0:T(8,128)(2,1)S(1)}, u32[]{:S(2)}) copy-start(bf16[256,1152]{1,0:T(8,128)(2,1)S(1)} %collective-permute-done.13.refs_4_) | copy-start | bytes 1769476
  182.4 3.8 %copy-start.15 = (bf16[256,1152]{1,0:T(8,128)(2,1)}, bf16[256,1152]{1,0:T(8,128)(2,1)S(1)}, u32[]{:S(2)}) copy-start(bf16[256,1152]{1,0:T(8,128)(2,1)S(1)} %collective-permute-done.14.refs_5_) | copy-start | bytes 1769476
  183.1 3.0 %collective-permute-start.15 = (bf16[256,1152]{1,0:T(8,128)(2,1)S(1)}, bf16[256,1152]{1,0:T(8,128)(2,1)S(1)}, u32[]{:S(2)}, u32[]{:S(2)}) collective-permute-start(bf16[256,1152]{1,0:T(8,128)(2,1)S(1)} %select_add_fusion.2), channel_id=1, source_target_pairs={{0,1},{1,0},{2,3},{3,2},{4,5},{5,4},{6,7},{7,6},{8,9},{9,8},{10,11... | collective-permute-start | bytes 1769480 | tf_op jit(solution)/shard_map/ppermute | solution.py:206
  (9 other events, 11.4 us)
where the time goes:
time: 199 us; the launch traced here: 196 us
  waiting for transfers between devices  66.8 us (34%)
  Pallas kernels  64.1 us (32%)
  local copies, waits for them, and re-layouts  25.2 us (13%)
  starting transfers between devices  23.7 us (12%)
  other arithmetic  14.8 us (7%)
    pallas_call x3, Pallas kernels, visit(): pl.pallas_call(functools.partial(visit_body, sizes, temp, last, len(waits...  39.8 us
    ppermute x2, waiting for transfers between devices, shards(): one = [lax.ppermute(piece, AXES, HALF_SWAP) for piece in pieces[:2]]  38.1 us
    pallas_call x2, Pallas kernels, own_gradient(): pl.pallas_call(functools.partial(own_body, temp, len(waits)), in_specs=[h...  24.4 us
    ppermute x1, waiting for transfers between devices, shards(): lax.ppermute(one[1], AXES, HAND_ON_WITHIN)  23.6 us
    unnamed x50, local copies, waits for them, and re-layouts  18.8 us
    concatenate x4, other arithmetic, shards(): jnp.concatenate([texts[at:at + size], images[at:at + size]], axis=0)  5.46 us
    add x3, other arithmetic, behind(): return array + token[0, 0].astype(array.dtype)  4.68 us
    select_n x1, other arithmetic, shards(): jnp.where(first_passes_on, one[1], two[1])  4.65 us
  transfers between devices with their start and end apart: 16, of which 5 were waited for; matrix products, arithmetic and copies ran while one was open for 10% of the time, Pallas kernels for 28%

commit v1 on v0

--- a/solution.py
+++ b/solution.py
@@ -101,8 +101,8 @@
     )(*in_hbm(rows, own, other), partner, *in_hbm(*waits))
 
 
-def visit_body(sizes, temp, last, waits, *refs):
-    count = len(sizes)
+def visit_body(sizes, temp, last, waits, split, *refs):
+    count = len(sizes) + split
     kept, before, others = refs[:2], refs[2:4], refs[4 : 4 + count]
     refs = refs[4 + count + waits :]
     out, (token, stack, weight, sems, *rest) = refs[:2], refs[2:]
@@ -111,14 +111,15 @@
     for side in (0, 1):
         at = 0
         for i, size in enumerate(sizes):
-            source = others[i].at[pl.ds(side * size, size)]
+            ref = others[i + side] if split and i == count - 2 else others[i]
+            source = ref if split and i == count - 2 else ref.at[pl.ds(side * size, size)]
             copies.append(pltpu.make_async_copy(source, stack.at[side, pl.ds(at, size)], sems.at[side, i]))
             at += size
     for copy in copies:
         copy.start()
     sent = []
     for side in (0, 1):
-        for copy in copies[side * count : (side + 1) * count]:
+        for copy in copies[side * len(sizes) : (side + 1) * len(sizes)]:
             copy.wait()
         for b in range(kept[side].shape[0] // BLOCK):
             here = slice(b * BLOCK, (b + 1) * BLOCK)
@@ -136,10 +137,12 @@
         copy.wait()
 
 
-def visit(kept, before, others, temp, last, waits):
+def visit(kept, before, others, temp, last, waits, split=False):
     height, width = kept[0].shape
     sizes = tuple(other.shape[0] // 2 for other in others)
-    many, count = sum(sizes), len(sizes)
+    if split:
+        sizes = sizes[:-2] + (others[-1].shape[0],)
+    many, count = sum(sizes), len(others)
     hbm, vmem = pl.BlockSpec(memory_space=pltpu.HBM), pl.BlockSpec(memory_space=pltpu.VMEM)
     kept = [pltpu.with_memory_space_constraint(array, pltpu.VMEM) for array in kept]
     before = [pltpu.with_memory_space_constraint(array, pltpu.VMEM) for array in before]
@@ -154,7 +157,7 @@
     else:
         out_shape = [pltpu.VMEM((height, width), jnp.float32)] * 2
     return pl.pallas_call(
-        functools.partial(visit_body, sizes, temp, last, len(waits)),
+        functools.partial(visit_body, sizes, temp, last, len(waits), split),
         in_specs=[vmem] * 4 + [hbm] * (count + len(waits)),
         out_specs=[hbm if last else vmem] * 2 + [vmem],
         out_shape=out_shape + [TOKEN],
@@ -200,9 +203,10 @@
     near = lax.ppermute(behind(jnp.where(first_passes_on, one[0], two[0]), token), AXES, CORE_SWAP)
     *totals, token = visit(kept, totals, [one[0], two[0], near], temp, False, (across[1],))
     near = lax.ppermute(behind(jnp.where(even, ahead[0], back[0]), token), AXES, CORE_SWAP)
-    two[1] = behind(two[1] + jnp.concatenate(across, axis=0), token)
-    far = lax.ppermute(jnp.where(first_passes_on, one[1], two[1]), AXES, CORE_SWAP)
-    *totals, token = visit(kept, totals, [ahead[0], back[0], near, one[1], two[1], far], temp, False, ())
+    handed = two[1] + jnp.concatenate(across, axis=0)
+    far = lax.ppermute(behind(jnp.where(first_passes_on, one[1], handed), token), AXES, CORE_SWAP)
+    others = [ahead[0], back[0], near, one[1], two[1], far, *across]
+    *totals, token = visit(kept, totals, others, temp, False, (), split=True)
     near = lax.ppermute(behind(jnp.where(even, ahead[1], back[1]), token), AXES, CORE_SWAP)
     *totals, token = visit(kept, totals, [ahead[1], back[1], near], temp, True, ())
     return tuple(totals)

time: 199 us -> 199 us (level)
  the two profiles are of different devices: /device:TPU:105 before, /device:TPU:1 now
where the time goes in v1:
time: 199 us; the launch traced here: 196 us
  Pallas kernels  65.3 us (33%)
  waiting for transfers between devices  44.6 us (22%)
  starting transfers between devices  44 us (22%)
  local copies, waits for them, and re-layouts  27.3 us (14%)
  other arithmetic  13.3 us (7%)
    pallas_call x3, Pallas kernels, visit(): pl.pallas_call(functools.partial(visit_body, sizes, temp, last, len(waits...  40.9 us
    pallas_call x2, Pallas kernels, own_gradient(): pl.pallas_call(functools.partial(own_body, temp, len(waits)), in_specs=[h...  24.4 us
    unnamed x50, local copies, waits for them, and re-layouts  20.9 us
    ppermute x2, starting transfers between devices, shards(): lax.ppermute(rows, AXES, ACROSS)  16 us
    ppermute x2, waiting for transfers between devices, shards(): one = [lax.ppermute(piece, AXES, HALF_SWAP) for piece in pieces[:2]]  14 us
    ppermute x2, waiting for transfers between devices, shards(): ahead = [lax.ppermute(piece, AXES, AHEAD) for piece in pieces[2:]]  13.1 us
    ppermute x2, waiting for transfers between devices, shards(): lax.ppermute(rows, AXES, ACROSS)  10.7 us
    ppermute x2, starting transfers between devices, shards(): ahead = [lax.ppermute(piece, AXES, AHEAD) for piece in pieces[2:]]  8.28 us
  transfers between devices with their start and end apart: 16, of which 6 were waited for; matrix products, arithmetic and copies ran while one was open for 10% of the time, Pallas kernels for 29%

profile of v1, /device:TPU:1, one launch (start us, length us, event | category | flops | bytes accessed | tf_op | source)
XLA Modules:
  0.0 195.6 jit_solution(4186157514325125249)
XLA Ops:
  2.2 2.2 %fusion.3 = (bf16[288,1152]{1,0:T(8,128)(2,1)S(1)}, bf16[288,1152]{1,0:T(8,128)(2,1)}) fusion(bf16[896,1152]{1,0:T(8,128)(2,1)} %rows.3), kind=kLoop, calls=%fused_computation.13 | loop fusion | bytes 2654208 | tf_op jit(solution)/shard_map/slice | solution.py:182
  5.8 3.0 %collective-permute-start.3 = (bf16[576,1152]{1,0:T(8,128)(2,1)}, bf16[576,1152]{1,0:T(8,128)(2,1)}, u32[]{:S(2)}, u32[]{:S(2)}) collective-permute-start(bf16[576,1152]{1,0:T(8,128)(2,1)} %pad_maximum_fusion), channel_id=1, source_target_pairs={{0,2},{1,3},{2,0},{3,1},{4,6},{5,7},{6,4},{7,5},{8,10},{9,11},{10,... | collective-permute-start | bytes 3981320 | tf_op jit(solution)/shard_map/ppermute | solution.py:187
  8.8 8.3 %collective-permute-start.2 = (bf16[288,1152]{1,0:T(8,128)(2,1)}, bf16[288,1152]{1,0:T(8,128)(2,1)}, u32[]{:S(2)}, u32[]{:S(2)}) collective-permute-start(bf16[288,1152]{1,0:T(8,128)(2,1)} %get-tuple-element.33), channel_id=1, source_target_pairs={{62,64},{63,65},{64,62},{65,63},{126,0},{127,1},{0,126},{1,127}} | collective-permute-start | bytes 1990664 | tf_op jit(solution)/shard_map/ppermute | solution.py:188
  17.2 2.4 %pad_maximum_fusion.1 = bf16[576,1152]{1,0:T(8,128)(2,1)} fusion(bf16[288,1152]{1,0:T(8,128)(2,1)S(1)} %get-tuple-element.30, bf16[288,1152]{1,0:T(8,128)(2,1)} %get-tuple-element.33), kind=kLoop, calls=%fused_computation.1 | loop fusion | flops 2654208 | bytes 2654208 | tf_op jit(solution)/shard_map/concatenate | solution.py:182
  24.0 14.0 %collective-permute-done.3.refs_4_ = bf16[576,1152]{1,0:T(8,128)(2,1)} collective-permute-done((bf16[576,1152]{1,0:T(8,128)(2,1)}, bf16[576,1152]{1,0:T(8,128)(2,1)}, u32[]{:S(2)}, u32[]{:S(2)}) %collective-permute-start.3) | collective-permute-done | bytes 1327136 | tf_op jit(solution)/shard_map/ppermute | solution.py:187
  39.4 12.0 %shard_map.59 = (f32[896,1152]{1,0:T(8,128)S(1)}, bf16[896,1152]{1,0:T(8,128)(2,1)S(1)}, f32[8,128]{1,0:T(8,128)S(1)}) custom-call(bf16[896,1152]{1,0:T(8,128)(2,1)} %own.3, bf16[896,1152]{1,0:T(8,128)(2,1)} %rows.3, bf16[896,1152]{1,0:T(8,128)(2,1)} %collective-permute-done.other, s32[896,1]{1,0:T(8,128)S(1)} %broadcast_in_dim.8.partner, ...), custom_call_target="tpu_custom_call" | custom-call | flops 7398752256 | bytes 6193152 | tf_op jit(solution)/shard_map/pallas_call | solution.py:83
  51.4 2.0 %copy-done = f32[896,1152]{1,0:T(8,128)} copy-done((f32[896,1152]{1,0:T(8,128)}, f32[896,1152]{1,0:T(8,128)S(1)}, u32[]{:S(2)}) %copy-start) | copy-done | bytes 4128792
  53.9 12.4 %shard_map.60 = (f32[896,1152]{1,0:T(8,128)S(1)}, bf16[896,1152]{1,0:T(8,128)(2,1)S(1)}, f32[8,128]{1,0:T(8,128)S(1)}) custom-call(bf16[896,1152]{1,0:T(8,128)(2,1)} %rows.3, bf16[896,1152]{1,0:T(8,128)(2,1)} %own.3, bf16[896,1152]{1,0:T(8,128)(2,1)} %collective-permute-done.1.other, s32[896,1]{1,0:T(8,128)S(1)} %broadcast_in_dim.9.partner, ...), custom_call_target="tpu_custom_call" | custom-call | flops 7398752256 | bytes 6193152 | tf_op jit(solution)/shard_map/pallas_call | solution.py:83
  66.4 2.0 %copy-done.4 = f32[896,1152]{1,0:T(8,128)} copy-done((f32[896,1152]{1,0:T(8,128)}, f32[896,1152]{1,0:T(8,128)S(1)}, u32[]{:S(2)}) %copy-start.4) | copy-done | bytes 4128792
  70.2 2.5 %collective-permute-done.4.refs_5_ = bf16[576,1152]{1,0:T(8,128)(2,1)S(1)} collective-permute-done((bf16[576,1152]{1,0:T(8,128)(2,1)}, bf16[576,1152]{1,0:T(8,128)(2,1)S(1)}, u32[]{:S(2)}, u32[]{:S(2)}) %collective-permute-start.4) | collective-permute-done | bytes 1327136 | tf_op jit(solution)/shard_map/ppermute | solution.py:199
  72.7 2.0 %select_add_fusion = bf16[576,1152]{1,0:T(8,128)(2,1)} fusion(bf16[576,1152]{1,0:T(8,128)(2,1)} %collective-permute-done.3.refs_4_, bf16[576,1152]{1,0:T(8,128)(2,1)S(1)} %collective-permute-done.4.refs_5_, pred[]{:T(512)S(6)} %eq.6, bf16[]{:T(256)} %bitcast), kind=kLoop, calls=%fused_computation.5 | loop fusion | flops 1327104 | bytes 3981315 | tf_op jit(solution)/shard_map/add | solution.py:73
  74.6 4.2 %collective-permute-start.5 = (bf16[576,1152]{1,0:T(8,128)(2,1)}, bf16[576,1152]{1,0:T(8,128)(2,1)}, u32[]{:S(2)}, u32[]{:S(2)}) collective-permute-start(bf16[576,1152]{1,0:T(8,128)(2,1)} %select_add_fusion), channel_id=1, source_target_pairs={{0,1},{1,0},{2,3},{3,2},{4,5},{5,4},{6,7},{7,6},{8,9},{9,8},{10,11... | collective-permute-start | bytes 3981320 | tf_op jit(solution)/shard_map/ppermute | solution.py:203
  78.8 7.7 %collective-permute-start.6 = (bf16[288,1152]{1,0:T(8,128)(2,1)S(1)}, bf16[288,1152]{1,0:T(8,128)(2,1)S(1)}, u32[]{:S(2)}, u32[]{:S(2)}) collective-permute-start(bf16[288,1152]{1,0:T(8,128)(2,1)S(1)} %copy-done.13), channel_id=1, source_target_pairs={{62,64},{63,65},{64,62},{65,63},{126,0},{127,1},{0,126},{1,127}} | collective-permute-start | bytes 1990664 | tf_op jit(solution)/shard_map/ppermute | solution.py:188
  86.5 2.5 %collective-permute-start.11 = (bf16[576,1152]{1,0:T(8,128)(2,1)}, bf16[576,1152]{1,0:T(8,128)(2,1)}, u32[]{:S(2)}, u32[]{:S(2)}) collective-permute-start(bf16[576,1152]{1,0:T(8,128)(2,1)} %collective-permute-done.10.refs_7_), channel_id=1, source_target_pairs={{0,4},{1,5},{4,8},{5,9},{6,2},{7,3},{8,12},{9,13},{10,6},{11,7},{1... | collective-permute-start | bytes 3981320 | tf_op jit(solution)/shard_map/ppermute | solution.py:199
  90.1 1.9 collective-permute-start.8
  91.9 10.7 %collective-permute-done.6.refs_7_.refs_11_ = bf16[288,1152]{1,0:T(8,128)(2,1)S(1)} collective-permute-done((bf16[288,1152]{1,0:T(8,128)(2,1)S(1)}, bf16[288,1152]{1,0:T(8,128)(2,1)S(1)}, u32[]{:S(2)}, u32[]{:S(2)}) %collective-permute-start.6) | collective-permute-done | bytes 663584 | tf_op jit(solution)/shard_map/ppermute | solution.py:188
  103.5 2.2 %copy-done.1 = f32[896,1152]{1,0:T(8,128)S(1)} copy-done((f32[896,1152]{1,0:T(8,128)S(1)}, f32[896,1152]{1,0:T(8,128)}, u32[]{:S(2)}) %copy-start.1) | copy-done | bytes 4128792
  105.7 2.2 %copy-done.5 = f32[896,1152]{1,0:T(8,128)S(1)} copy-done((f32[896,1152]{1,0:T(8,128)S(1)}, f32[896,1152]{1,0:T(8,128)}, u32[]{:S(2)}) %copy-start.5) | copy-done | bytes 4128792
  109.4 11.6 %shard_map.61 = (f32[896,1152]{1,0:T(8,128)S(1)}, f32[896,1152]{1,0:T(8,128)S(1)}, f32[8,128]{1,0:T(8,128)S(1)}) custom-call(bf16[896,1152]{1,0:T(8,128)(2,1)S(1)} %get-tuple-element.16.refs_0_, bf16[896,1152]{1,0:T(8,128)(2,1)S(1)} %copy-done.9, f32[896,1152]{1,0:T(8,128)S(1)} %copy-done.1, ...), custom_call_target="tpu_custom_call", output_to_operand_aliasing={{0}: (2, {}), {1}: (3, {})} | custom-call | flops 7134511104 | bytes 3981312 | tf_op jit(solution)/shard_map/pallas_call | solution.py:159
  121.1 2.0 %copy-done.2 = f32[896,1152]{1,0:T(8,128)} copy-done((f32[896,1152]{1,0:T(8,128)}, f32[896,1152]{1,0:T(8,128)S(1)}, u32[]{:S(2)}) %copy-start.2) | copy-done | bytes 4128792
  123.0 2.0 %copy-done.6 = f32[896,1152]{1,0:T(8,128)} copy-done((f32[896,1152]{1,0:T(8,128)}, f32[896,1152]{1,0:T(8,128)S(1)}, u32[]{:S(2)}) %copy-start.6) | copy-done | bytes 4128792
  125.6 3.2 %fusion.1 = bf16[576,1152]{1,0:T(8,128)(2,1)S(1)} fusion(bf16[576,1152]{1,0:T(8,128)(2,1)} %collective-permute-done.10.refs_7_, bf16[576,1152]{1,0:T(8,128)(2,1)} %collective-permute-done.11.refs_8_, bf16[288,1152]{1,0:T(8,128)(2,1)} %copy-done.18, bf16[288,1152]{1,0:T(8,128)(2,1)} %collective-permute-done.2.refs_1_.refs_10_, pred[]{:T(512)S(6)} %eq.6, ...), kind=kLoop, calls=%fused_computation.4 | loop fusion | flops 7299072 | bytes 5308419 | tf_op jit(solution)/shard_map/add | solution.py:73
  128.8 1.8 collective-permute-start.12
  130.6 13.1 %collective-permute-done.7.refs_4_ = bf16[384,1152]{1,0:T(8,128)(2,1)} collective-permute-done((bf16[384,1152]{1,0:T(8,128)(2,1)}, bf16[384,1152]{1,0:T(8,128)(2,1)}, u32[]{:S(2)}, u32[]{:S(2)}) %collective-permute-start.7) | collective-permute-done | bytes 884768 | tf_op jit(solution)/shard_map/ppermute | solution.py:200
  143.7 1.9 select_add_fusion.1
  146.9 7.2 %collective-permute-start.13 = (bf16[256,1152]{1,0:T(8,128)(2,1)S(1)}, bf16[256,1152]{1,0:T(8,128)(2,1)S(1)}, u32[]{:S(2)}, u32[]{:S(2)}) collective-permute-start(bf16[256,1152]{1,0:T(8,128)(2,1)S(1)} %copy-done.20), channel_id=1, source_target_pairs={{0,126},{1,127},{2,0},{3,1},{4,2},{5,3},{6,4},{7,5},{8,6},{9,7},{1... | collective-permute-start | bytes 1769480 | tf_op jit(solution)/shard_map/ppermute | solution.py:200
  155.4 2.2 %copy-done.7 = f32[896,1152]{1,0:T(8,128)S(1)} copy-done((f32[896,1152]{1,0:T(8,128)S(1)}, f32[896,1152]{1,0:T(8,128)}, u32[]{:S(2)}) %copy-start.7) | copy-done | bytes 4128792
  157.6 20.8 %shard_map.62 = (f32[896,1152]{1,0:T(8,128)S(1)}, f32[896,1152]{1,0:T(8,128)S(1)}, f32[8,128]{1,0:T(8,128)S(1)}) custom-call(bf16[896,1152]{1,0:T(8,128)(2,1)S(1)} %get-tuple-element.16.refs_0_, bf16[896,1152]{1,0:T(8,128)(2,1)S(1)} %copy-done.10, f32[896,1152]{1,0:T(8,128)S(1)} %copy-done.3, ...), custom_call_target="tpu_custom_call", output_to_operand_aliasing={{0}: (2, {}), {1}: (3, {})} | custom-call | flops 14269022208 | bytes 7962624 | tf_op jit(solution)/shard_map/pallas_call | solution.py:159
  178.9 2.7 %collective-permute-done.14.refs_5_ = bf16[256,1152]{1,0:T(8,128)(2,1)S(1)} collective-permute-done((bf16[256,1152]{1,0:T(8,128)(2,1)S(1)}, bf16[256,1152]{1,0:T(8,128)(2,1)S(1)}, u32[]{:S(2)}, u32[]{:S(2)}) %collective-permute-start.14) | collective-permute-done | bytes 589856 | tf_op jit(solution)/shard_map/ppermute | solution.py:201
  182.3 2.1 %collective-permute-start.15 = (bf16[256,1152]{1,0:T(8,128)(2,1)S(1)}, bf16[256,1152]{1,0:T(8,128)(2,1)S(1)}, u32[]{:S(2)}, u32[]{:S(2)}) collective-permute-start(bf16[256,1152]{1,0:T(8,128)(2,1)S(1)} %select_add_fusion.2), channel_id=1, source_target_pairs={{0,1},{1,0},{2,3},{3,2},{4,5},{5,4},{6,7},{7,6},{8,9},{9,8},{10,11... | collective-permute-start | bytes 1769480 | tf_op jit(solution)/shard_map/ppermute | solution.py:210
  184.4 1.6 collective-permute-done.15.refs_6_
  186.8 8.5 %shard_map.63 = (f32[896,1152]{1,0:T(8,128)}, f32[896,1152]{1,0:T(8,128)}, f32[8,128]{1,0:T(8,128)}) custom-call(bf16[896,1152]{1,0:T(8,128)(2,1)S(1)} %get-tuple-element.16.refs_0_, bf16[896,1152]{1,0:T(8,128)(2,1)S(1)} %copy-done.10, f32[896,1152]{1,0:T(8,128)S(1)} %get-tuple-element.25.refs_2_, f32[896,1152]{1,0:T(8,128)S(1)} %get-tuple-element.26.refs_3_, ...), custom_call_target="tpu_custom_call" | custom-call | flops 3170893824 | bytes 1769472 | tf_op jit(solution)/shard_map/pallas_call | solution.py:159
  (79 shorter events, 19.9 us)
Async XLA Ops:
  0.6 3.8 %copy-start.16 = (bf16[896,1152]{1,0:T(8,128)(2,1)S(1)}, bf16[896,1152]{1,0:T(8,128)(2,1)}, u32[]{:S(2)}) copy-start(bf16[896,1152]{1,0:T(8,128)(2,1)} %own.3) | copy-start | bytes 6193156
  0.6 38.7 %collective-permute-start = (bf16[896,1152]{1,0:T(8,128)(2,1)}, bf16[896,1152]{1,0:T(8,128)(2,1)}, u32[]{:S(2)}, u32[]{:S(2)}) collective-permute-start(bf16[896,1152]{1,0:T(8,128)(2,1)} %rows.3), channel_id=1, source_target_pairs={{0,1},{1,0},{2,3},{3,2},{4,5},{5,4},{6,7},{7,6},{8,9},{9,8},{10,11... | collective-permute-start | bytes 6193160 | tf_op jit(solution)/shard_map/ppermute | solution.py:185
  2.1 51.8 %collective-permute-start.1 = (bf16[896,1152]{1,0:T(8,128)(2,1)}, bf16[896,1152]{1,0:T(8,128)(2,1)}, u32[]{:S(2)}, u32[]{:S(2)}) collective-permute-start(bf16[896,1152]{1,0:T(8,128)(2,1)} %own.3), channel_id=1, source_target_pairs={{0,1},{1,0},{2,3},{3,2},{4,5},{5,4},{6,7},{7,6},{8,9},{9,8},{10,11... | collective-permute-start | bytes 6193160 | tf_op jit(solution)/shard_map/ppermute | solution.py:186
  4.6 15.0 %copy-start.12 = (bf16[288,1152]{1,0:T(8,128)(2,1)}, bf16[288,1152]{1,0:T(8,128)(2,1)S(1)}, u32[]{:S(2)}) copy-start(bf16[288,1152]{1,0:T(8,128)(2,1)S(1)} %get-tuple-element.30) | copy-start | bytes 1990660
  5.8 32.1 %collective-permute-start.3 = (bf16[576,1152]{1,0:T(8,128)(2,1)}, bf16[576,1152]{1,0:T(8,128)(2,1)}, u32[]{:S(2)}, u32[]{:S(2)}) collective-permute-start(bf16[576,1152]{1,0:T(8,128)(2,1)} %pad_maximum_fusion), channel_id=1, source_target_pairs={{0,2},{1,3},{2,0},{3,1},{4,6},{5,7},{6,4},{7,5},{8,10},{9,11},{10,... | collective-permute-start | bytes 3981320 | tf_op jit(solution)/shard_map/ppermute | solution.py:187
  8.8 45.1 %collective-permute-start.2 = (bf16[288,1152]{1,0:T(8,128)(2,1)}, bf16[288,1152]{1,0:T(8,128)(2,1)}, u32[]{:S(2)}, u32[]{:S(2)}) collective-permute-start(bf16[288,1152]{1,0:T(8,128)(2,1)} %get-tuple-element.33), channel_id=1, source_target_pairs={{62,64},{63,65},{64,62},{65,63},{126,0},{127,1},{0,126},{1,127}} | collective-permute-start | bytes 1990664 | tf_op jit(solution)/shard_map/ppermute | solution.py:188
  19.6 2.2 %copy-start.21 = (s32[896]{0:T(1024)S(1)}, s32[896]{0:T(1024)}, u32[]{:S(2)}) copy-start(s32[896]{0:T(1024)} %param.6) | copy-start | bytes 10756
  19.6 2.4 %copy-start.22 = (s32[896]{0:T(1024)S(1)}, s32[896]{0:T(1024)}, u32[]{:S(2)}) copy-start(s32[896]{0:T(1024)} %param.7) | copy-start | bytes 10756
  19.6 66.9 %collective-permute-start.10 = (bf16[576,1152]{1,0:T(8,128)(2,1)}, bf16[576,1152]{1,0:T(8,128)(2,1)}, u32[]{:S(2)}, u32[]{:S(2)}) collective-permute-start(bf16[576,1152]{1,0:T(8,128)(2,1)} %pad_maximum_fusion.1), channel_id=1, source_target_pairs={{0,2},{1,3},{2,0},{3,1},{4,6},{5,7},{6,4},{7,5},{8,10},{9,11},{10,... | collective-permute-start | bytes 3981320 | tf_op jit(solution)/shard_map/ppermute | solution.py:187
  38.0 34.7 %collective-permute-start.4 = (bf16[576,1152]{1,0:T(8,128)(2,1)}, bf16[576,1152]{1,0:T(8,128)(2,1)S(1)}, u32[]{:S(2)}, u32[]{:S(2)}) collective-permute-start(bf16[576,1152]{1,0:T(8,128)(2,1)} %collective-permute-done.3.refs_4_), channel_id=1, source_target_pairs={{0,4},{1,5},{2,126},{3,127},{4,8},{5,9},{6,2},{7,3},{8,12},{9,13},... | collective-permute-start | bytes 3981320 | tf_op jit(solution)/shard_map/ppermute | solution.py:199
  51.3 2.0 %copy-start = (f32[896,1152]{1,0:T(8,128)}, f32[896,1152]{1,0:T(8,128)S(1)}, u32[]{:S(2)}) copy-start(f32[896,1152]{1,0:T(8,128)S(1)} %get-tuple-element.19.refs_2_) | copy-start | bytes 12386308
  66.3 2.0 %copy-start.4 = (f32[896,1152]{1,0:T(8,128)}, f32[896,1152]{1,0:T(8,128)S(1)}, u32[]{:S(2)}) copy-start(f32[896,1152]{1,0:T(8,128)S(1)} %get-tuple-element.20.refs_3_) | copy-start | bytes 12386308
  72.7 6.1 %copy-start.13 = (bf16[288,1152]{1,0:T(8,128)(2,1)S(1)}, bf16[288,1152]{1,0:T(8,128)(2,1)}, u32[]{:S(2)}) copy-start(bf16[288,1152]{1,0:T(8,128)(2,1)} %copy-done.12) | copy-start | bytes 1990660
  74.6 28.0 %collective-permute-start.5 = (bf16[576,1152]{1,0:T(8,128)(2,1)}, bf16[576,1152]{1,0:T(8,128)(2,1)}, u32[]{:S(2)}, u32[]{:S(2)}) collective-permute-start(bf16[576,1152]{1,0:T(8,128)(2,1)} %select_add_fusion), channel_id=1, source_target_pairs={{0,1},{1,0},{2,3},{3,2},{4,5},{5,4},{6,7},{7,6},{8,9},{9,8},{10,11... | collective-permute-start | bytes 3981320 | tf_op jit(solution)/shard_map/ppermute | solution.py:203
  78.8 23.8 %collective-permute-start.6 = (bf16[288,1152]{1,0:T(8,128)(2,1)S(1)}, bf16[288,1152]{1,0:T(8,128)(2,1)S(1)}, u32[]{:S(2)}, u32[]{:S(2)}) collective-permute-start(bf16[288,1152]{1,0:T(8,128)(2,1)S(1)} %copy-done.13), channel_id=1, source_target_pairs={{62,64},{63,65},{64,62},{65,63},{126,0},{127,1},{0,126},{1,127}} | collective-permute-start | bytes 1990664 | tf_op jit(solution)/shard_map/ppermute | solution.py:188
  86.5 39.1 %collective-permute-start.11 = (bf16[576,1152]{1,0:T(8,128)(2,1)}, bf16[576,1152]{1,0:T(8,128)(2,1)}, u32[]{:S(2)}, u32[]{:S(2)}) collective-permute-start(bf16[576,1152]{1,0:T(8,128)(2,1)} %collective-permute-done.10.refs_7_), channel_id=1, source_target_pairs={{0,4},{1,5},{4,8},{5,9},{6,2},{7,3},{8,12},{9,13},{10,6},{11,7},{1... | collective-permute-start | bytes 3981320 | tf_op jit(solution)/shard_map/ppermute | solution.py:199
  89.0 54.7 %collective-permute-start.7 = (bf16[384,1152]{1,0:T(8,128)(2,1)}, bf16[384,1152]{1,0:T(8,128)(2,1)}, u32[]{:S(2)}, u32[]{:S(2)}) collective-permute-start(bf16[384,1152]{1,0:T(8,128)(2,1)} %pad_maximum_fusion.2.refs_0_), channel_id=1, source_target_pairs={{0,126},{1,127},{2,0},{3,1},{4,2},{5,3},{6,4},{7,5},{8,6},{9,7},{1... | collective-permute-start | bytes 2654216 | tf_op jit(solution)/shard_map/ppermute | solution.py:200
  90.1 53.6 %collective-permute-start.8 = (bf16[384,1152]{1,0:T(8,128)(2,1)}, bf16[384,1152]{1,0:T(8,128)(2,1)}, u32[]{:S(2)}, u32[]{:S(2)}) collective-permute-start(bf16[384,1152]{1,0:T(8,128)(2,1)} %pad_maximum_fusion.2.refs_0_), channel_id=1, source_target_pairs={{0,2},{1,3},{2,4},{3,5},{4,6},{5,7},{6,8},{7,9},{8,10},{9,11},{10,... | collective-permute-start | bytes 2654216 | tf_op jit(solution)/shard_map/ppermute | solution.py:201
  103.5 2.2 %copy-start.1 = (f32[896,1152]{1,0:T(8,128)S(1)}, f32[896,1152]{1,0:T(8,128)}, u32[]{:S(2)}) copy-start(f32[896,1152]{1,0:T(8,128)} %copy-done) | copy-start | bytes 12386308
  105.7 2.2 %copy-start.5 = (f32[896,1152]{1,0:T(8,128)S(1)}, f32[896,1152]{1,0:T(8,128)}, u32[]{:S(2)}) copy-start(f32[896,1152]{1,0:T(8,128)} %copy-done.4) | copy-start | bytes 12386308
  121.1 2.0 %copy-start.2 = (f32[896,1152]{1,0:T(8,128)}, f32[896,1152]{1,0:T(8,128)S(1)}, u32[]{:S(2)}) copy-start(f32[896,1152]{1,0:T(8,128)S(1)} %get-tuple-element.22.refs_2_) | copy-start | bytes 12386308
  125.6 29.8 %copy-start.3 = (f32[896,1152]{1,0:T(8,128)S(1)}, f32[896,1152]{1,0:T(8,128)}, u32[]{:S(2)}) copy-start(f32[896,1152]{1,0:T(8,128)} %copy-done.2) | copy-start | bytes 12386308
  128.8 18.1 %copy-start.20 = (bf16[256,1152]{1,0:T(8,128)(2,1)S(1)}, bf16[256,1152]{1,0:T(8,128)(2,1)}, u32[]{:S(2)}) copy-start(bf16[256,1152]{1,0:T(8,128)(2,1)} %pad_maximum_fusion.3.refs_1_) | copy-start | bytes 1769476
  128.8 26.6 %copy-start.10 = (bf16[896,1152]{1,0:T(8,128)(2,1)S(1)}, bf16[896,1152]{1,0:T(8,128)(2,1)}, u32[]{:S(2)}) copy-start(bf16[896,1152]{1,0:T(8,128)(2,1)} %copy-done.8) | copy-start | bytes 6193156
  128.8 25.3 %collective-permute-start.12 = (bf16[576,1152]{1,0:T(8,128)(2,1)S(1)}, bf16[576,1152]{1,0:T(8,128)(2,1)S(1)}, u32[]{:S(2)}, u32[]{:S(2)}) collective-permute-start(bf16[576,1152]{1,0:T(8,128)(2,1)S(1)} %fusion.1), channel_id=1, source_target_pairs={{0,1},{1,0},{2,3},{3,2},{4,5},{5,4},{6,7},{7,6},{8,9},{9,8},{10,11... | collective-permute-start | bytes 3981320 | tf_op jit(solution)/shard_map/ppermute | solution.py:207
  145.6 8.4 %collective-permute-start.9 = (bf16[384,1152]{1,0:T(8,128)(2,1)S(1)}, bf16[384,1152]{1,0:T(8,128)(2,1)S(1)}, u32[]{:S(2)}, u32[]{:S(2)}) collective-permute-start(bf16[384,1152]{1,0:T(8,128)(2,1)S(1)} %select_add_fusion.1), channel_id=1, source_target_pairs={{0,1},{1,0},{2,3},{3,2},{4,5},{5,4},{6,7},{7,6},{8,9},{9,8},{10,11... | collective-permute-start | bytes 2654216 | tf_op jit(solution)/shard_map/ppermute | solution.py:205
  146.9 32.0 %collective-permute-start.13 = (bf16[256,1152]{1,0:T(8,128)(2,1)S(1)}, bf16[256,1152]{1,0:T(8,128)(2,1)S(1)}, u32[]{:S(2)}, u32[]{:S(2)}) collective-permute-start(bf16[256,1152]{1,0:T(8,128)(2,1)S(1)} %copy-done.20), channel_id=1, source_target_pairs={{0,126},{1,127},{2,0},{3,1},{4,2},{5,3},{6,4},{7,5},{8,6},{9,7},{1... | collective-permute-start | bytes 1769480 | tf_op jit(solution)/shard_map/ppermute | solution.py:200
  154.1 27.5 %collective-permute-start.14 = (bf16[256,1152]{1,0:T(8,128)(2,1)S(1)}, bf16[256,1152]{1,0:T(8,128)(2,1)S(1)}, u32[]{:S(2)}, u32[]{:S(2)}) collective-permute-start(bf16[256,1152]{1,0:T(8,128)(2,1)S(1)} %copy-done.20), channel_id=1, source_target_pairs={{0,2},{1,3},{2,4},{3,5},{4,6},{5,7},{6,8},{7,9},{8,10},{9,11},{10,... | collective-permute-start | bytes 1769480 | tf_op jit(solution)/shard_map/ppermute | solution.py:201
  155.4 2.2 %copy-start.7 = (f32[896,1152]{1,0:T(8,128)S(1)}, f32[896,1152]{1,0:T(8,128)}, u32[]{:S(2)}) copy-start(f32[896,1152]{1,0:T(8,128)} %copy-done.6) | copy-start | bytes 12386308
  178.9 7.2 %copy-start.14 = (bf16[256,1152]{1,0:T(8,128)(2,1)}, bf16[256,1152]{1,0:T(8,128)(2,1)S(1)}, u32[]{:S(2)}) copy-start(bf16[256,1152]{1,0:T(8,128)(2,1)S(1)} %collective-permute-done.13.refs_4_) | copy-start | bytes 1769476
  181.6 4.5 %copy-start.15 = (bf16[256,1152]{1,0:T(8,128)(2,1)}, bf16[256,1152]{1,0:T(8,128)(2,1)S(1)}, u32[]{:S(2)}) copy-start(bf16[256,1152]{1,0:T(8,128)(2,1)S(1)} %collective-permute-done.14.refs_5_) | copy-start | bytes 1769476
  182.3 3.7 %collective-permute-start.15 = (bf16[256,1152]{1,0:T(8,128)(2,1)S(1)}, bf16[256,1152]{1,0:T(8,128)(2,1)S(1)}, u32[]{:S(2)}, u32[]{:S(2)}) collective-permute-start(bf16[256,1152]{1,0:T(8,128)(2,1)S(1)} %select_add_fusion.2), channel_id=1, source_target_pairs={{0,1},{1,0},{2,3},{3,2},{4,5},{5,4},{6,7},{7,6},{8,9},{9,8},{10,11... | collective-permute-start | bytes 1769480 | tf_op jit(solution)/shard_map/ppermute | solution.py:210
  (9 other events, 11.3 us)
